TPU v7x, 32 devices: a whole 2x2x4 slice. The times are simulated.
32 devices in a mesh: groups: 2 (over y), row: 4 (over z), col: 4 (over x, core).
Axes of the slice: x: 2, y: 2, z: 4, core: 2. Of those that a mesh axis runs over, the one named last changes fastest.
Arguments:
- tokens: bfloat16 [1024, 4096], P(('groups', 'row'), 'col'), parts along dimension 0, may hold values from -90 to 90
- norm_gain: float32 [4096], P('col'), may hold values from 0.5 to 1.5
- gate_weight: bfloat16 [4096, 16384], P('col', 'row'), may hold values from -0.09375 to 0.09375
- up_weight: bfloat16 [4096, 16384], P('col', 'row'), may hold values from -0.09375 to 0.09375
- down_weight: bfloat16 [16384, 4096], P('row', 'col'), may hold values from -0.046875 to 0.046875
Outputs:
- block_out: bfloat16 [1024, 4096], P(('groups', 'row'), 'col'), parts along dimension 0
There are 2 independent parts, one for each index of `groups`. A program takes and returns all parts, laid end to end along the dimension named above; an argument that names none is the same for every part. Nothing has to cross between parts.
All inputs are finite; a program needn't handle non-finite values.
Results may differ from a plain program's by a relative error of at most 0.02.
Values may be sent and summed in bfloat16 or wider, within the bound.
A program may use at most 128 MiB of HBM per device.

v0:
```python
import jax
import jax.numpy as jnp
from jax import lax
from jax.sharding import PartitionSpec as P

epsilon = 1e-05


def normalize(source, total_squares, width_total, norm_gain):
    inverse_rms = lax.rsqrt(total_squares / width_total + epsilon)
    return (source.astype(jnp.float32) * inverse_rms[:, None] * norm_gain[None, :]).astype(
        jnp.bfloat16
    )


def per_device(tokens, norm_gain, gate_weight, up_weight, down_weight):
    width_total = tokens.shape[1] * lax.axis_size("col")
    split_at = gate_weight.shape[1]
    both_weights = jnp.concatenate([gate_weight, up_weight], axis=1)
    local_squares = jnp.sum(jnp.square(tokens.astype(jnp.float32)), axis=1)
    total_squares = lax.psum(local_squares, "col")
    normed = normalize(tokens, total_squares, width_total, norm_gain)
    gathered = lax.all_gather(normed, "row", axis=0, tiled=True)
    block_rows = gathered
    summed = lax.psum_scatter(
        jnp.dot(block_rows, both_weights, preferred_element_type=jnp.float32).astype(jnp.bfloat16),
        "col",
        scatter_dimension=0,
        tiled=True,
    ).astype(jnp.float32)
    hidden_part = (jax.nn.silu(summed[:, :split_at]) * summed[:, split_at:]).astype(jnp.bfloat16)
    hidden = lax.all_gather(hidden_part, "col", axis=0, tiled=True)
    block_rows = hidden
    return lax.psum_scatter(
        jnp.dot(block_rows, down_weight, preferred_element_type=jnp.float32).astype(jnp.bfloat16),
        "row",
        scatter_dimension=0,
        tiled=True,
    )


def solution(mesh):
    placed = (
        P(("groups", "row"), "col"),
        P("col"),
        P("col", "row"),
        P("col", "row"),
        P("row", "col"),
    )
    return jax.shard_map(
        per_device,
        mesh=mesh,
        in_specs=placed,
        out_specs=P(("groups", "row"), "col"),
        check_vma=False,
    )
```

profile of v0, /device:TPU:0, one launch (start us, length us, event | category | flops | bytes accessed | tf_op | source)
XLA Modules:
  0.0 214.6 jit_solution(8213113644927217040)
XLA Ops:
  6.5 0.0 all-gather.3.cloned.1.call-start
  6.5 1.1 fusion.8
  7.6 8.3 %psum.7 = f32[128]{0:T(128)S(1)} all-reduce(f32[128]{0:T(128)S(1)} %fusion.8), channel_id=1, replica_groups=mesh['groups'=2,'row'=4,'col'=4] {'col'}, use_global_device_ids=true, to_apply=%region_1.0 | all-reduce | flops 128 | bytes 1024 | tf_op jit(solution)/shard_map/psum | solution.py:21
  16.0 1.8 fusion.10
  17.8 0.0 all-gather.3.cloned.1.call-update
  17.8 0.0 reduce-scatter.3.cloned.1.call-start
  17.8 28.4 %all-gather.3.cloned.1.call-done = bf16[512,1024]{1,0:T(8,128)(2,1)} async-done(((bf16[128,1024]{1,0:T(8,128)(2,1)}), bf16[512,1024]{1,0:T(8,128)(2,1)}) %all-gather.3.cloned.1.call-update) | async-done | bytes 1048592 | tf_op jit(solution)/shard_map/all_gather | solution.py:23
  46.2 14.8 %fusion.4 = bf16[512,8192]{1,0:T(8,128)(2,1)} fusion(bf16[512,1024]{1,0:T(8,128)(2,1)} %all-gather.3.cloned.1.call-done, bf16[1024,4096]{1,0:T(8,128)(2,1)} %param.8, bf16[1024,4096]{1,0:T(8,128)(2,1)} %param.7), kind=kOutput, calls=%fused_computation.4 | convolution fusion | flops 8627683328 | bytes 26214400 | tf_op jit(solution)/shard_map/dot_general | solution.py:26
  61.0 0.0 reduce-scatter.3.cloned.1.call-update
  61.0 0.0 all-gather.5.cloned.1.call-start
  61.0 71.3 %reduce-scatter.3.cloned.1.call-done = bf16[128,8192]{1,0:T(8,128)(2,1)} async-done(((bf16[512,8192]{1,0:T(8,128)(2,1)}), bf16[128,8192]{1,0:T(8,128)(2,1)}) %reduce-scatter.3.cloned.1.call-update) | async-done | bytes 2097168 | tf_op jit(solution)/shard_map/reduce_scatter | solution.py:25
  132.4 2.0 convert_element_type.22
  134.4 1.5 fusion.7
  135.9 0.0 all-gather.5.cloned.1.call-update
  135.9 0.0 reduce-scatter.5.cloned.1.call-start
  136.0 34.6 %all-gather.5.cloned.1.call-done = bf16[512,4096]{1,0:T(8,128)(2,1)} async-done(((bf16[128,4096]{1,0:T(8,128)(2,1)}), bf16[512,4096]{1,0:T(8,128)(2,1)}) %all-gather.5.cloned.1.call-update) | async-done | bytes 4194320 | tf_op jit(solution)/shard_map/all_gather | solution.py:32
  170.6 10.1 %convolution_convert_fusion = bf16[512,1024]{1,0:T(8,128)(2,1)} fusion(bf16[512,4096]{1,0:T(8,128)(2,1)} %all-gather.5.cloned.1.call-done, bf16[4096,1024]{1,0:T(8,128)(2,1)} %param.9), kind=kOutput, calls=%fused_computation.7 | convolution fusion | flops 4295491584 | bytes 13631488 | tf_op jit(solution)/shard_map/dot_general | solution.py:35
  180.7 0.0 reduce-scatter.5.cloned.1.call-update
  180.7 27.3 %reduce-scatter.5.cloned.1.call-done = bf16[128,1024]{1,0:T(8,128)(2,1)} async-done(((bf16[512,1024]{1,0:T(8,128)(2,1)}), bf16[128,1024]{1,0:T(8,128)(2,1)}) %reduce-scatter.5.cloned.1.call-update) | async-done | bytes 262160 | tf_op jit(solution)/shard_map/reduce_scatter | solution.py:34
  (1 shorter events, 0.0 us)
Async XLA Ops:
  6.5 39.7 %all-gather.3.cloned.1.call-start = ((), (), s32[]{:S(2)}) async-start(), calls=%async_computation.2 | async-start | bytes 1310720 | tf_op jit(solution)/shard_map/all_gather | solution.py:23
  17.8 114.6 %reduce-scatter.3.cloned.1.call-start = ((), (), s32[]{:S(2)}) async-start(), calls=%async_computation.3 | async-start | bytes 10485760 | tf_op jit(solution)/shard_map/reduce_scatter | solution.py:25
  61.0 109.6 %all-gather.5.cloned.1.call-start = ((), (), s32[]{:S(2)}) async-start(), calls=%async_computation.4 | async-start | bytes 5242880 | tf_op jit(solution)/shard_map/all_gather | solution.py:32
  135.9 72.1 %reduce-scatter.5.cloned.1.call-start = ((), (), s32[]{:S(2)}) async-start(), calls=%async_computation.5 | async-start | bytes 1310720 | tf_op jit(solution)/shard_map/reduce_scatter | solution.py:34
Sparse Core Ops, SparseCore 0:
  17.9 28.2 all-gather.2
  61.1 71.2 reduce-scatter.2
  136.1 34.4 all-gather.4
  180.9 27.1 reduce-scatter.4
where the time goes:
time: 215 us
  waiting for transfers between devices  162 us (75%)
  matrix products  24.9 us (12%)
  between operations  13.1 us (6%)
  blocking collectives  8.34 us (4%)
  other arithmetic  6.43 us (3%)
    reduce_scatter x1, waiting for transfers between devices, per_device(): lax.psum_scatter(jnp.dot(block_rows, both_weights, preferred_element_type...  71.3 us
    all_gather x1, waiting for transfers between devices, per_device(): hidden = lax.all_gather(hidden_part, 'col', axis=0, tiled=True)  34.6 us
    all_gather x1, waiting for transfers between devices, per_device(): gathered = lax.all_gather(normed, 'row', axis=0, tiled=True)  28.4 us
    reduce_scatter x1, waiting for transfers between devices, per_device(): lax.psum_scatter(jnp.dot(block_rows, down_weight, preferred_element_type=...  27.3 us
    dot_general x1, matrix products, per_device(): jnp.dot(block_rows, both_weights, preferred_element_type=jnp.float32)  14.8 us
    dot_general x1, matrix products, per_device(): jnp.dot(block_rows, down_weight, preferred_element_type=jnp.float32)  10.1 us
    psum x1, blocking collectives, per_device(): total_squares = lax.psum(local_squares, 'col')  8.34 us
  transfers between devices with their start and end apart: 4, of which 4 were waited for; matrix products, arithmetic and copies ran while one was open for 0% of the time, Pallas kernels for 0%

commit v1 on v0

v1 whole, which is shorter than its diff:
```python
import functools
import jax
import jax.numpy as jnp
from jax import lax
from jax.experimental import pallas as pl
from jax.experimental.pallas import tpu as pltpu
from jax.sharding import PartitionSpec as P

epsilon = 1e-05
MESH = pl.DeviceIdType.MESH
f32 = jnp.float32
bf16 = jnp.bfloat16


def remote(src, dst, send, recv, device):
    return pltpu.make_async_remote_copy(
        src_ref=src, dst_ref=dst, send_sem=send, recv_sem=recv, device_id=device, device_id_type=MESH
    )


def kernel(n, width_total, tok, gain, gate_w, up_w, down_w, out,
           w_v, wd_v, xg, a_s, a_r, b_s, b_r, p_own, p_b, hid, q_s, q_r, o_s, o_r,
           w_sem, own_sem, t_ss, t_rs, a_ss, a_rs, b_ss, b_rs, h_ss, h_rs, q_ss, q_rs, o_ss, o_rs):
    T, width = tok.shape
    F = gate_w.shape[1] // 4
    tile_f = min(256, F)
    tile_d = min(256, width)
    row = lax.axis_index("row")
    col = lax.axis_index("col")
    hi, lo = col // 2, col % 2
    sibling = hi * 2 + (1 - lo)
    across = (1 - hi) * 2 + lo
    diagonal = (1 - hi) * 2 + (1 - lo)
    shards = (diagonal, across, sibling, col)

    def row_at(step):
        return lax.rem(row + step, n)

    def row_back(step):
        return lax.rem(row + n - step, n)

    def load(role, g):
        at = pl.ds(pl.multiple_of(shards[role] * F, F), F)
        source = (gate_w, up_w)[g].at[:, at]
        return pltpu.make_async_copy(source, w_v.at[role, g], w_sem.at[g, role])

    def load_down(role):
        at = pl.ds(pl.multiple_of(shards[role] * F, F), F)
        return pltpu.make_async_copy(down_w.at[at, :], wd_v.at[role], w_sem.at[2, role])

    def send_tokens(i):
        return remote(tok, xg.at[i], t_ss.at[i], t_rs.at[i], {"row": row_back(i)})

    def send_half(i, which):
        return remote(a_s.at[i, which], a_r.at[i, which], a_ss.at[i, which], a_rs.at[i, which], {"col": sibling})

    def send_chip(i):
        return remote(b_s.at[i], b_r.at[i], b_ss.at[i], b_rs.at[i], {"col": across})

    def send_hidden(i, which):
        source, target, device = ((3, 1, across), (3, 2, sibling), (1, 0, sibling))[which]
        return remote(hid.at[i, source], hid.at[i, target], h_ss.at[i, which], h_rs.at[i, which], {"col": device})

    def send_squares(i, role):
        return remote(q_s.at[i], q_r.at[i, role], q_ss.at[i, role], q_rs.at[i, role], {"col": shards[role]})

    def send_out(i):
        return remote(o_s.at[i], o_r.at[i], o_ss.at[i], o_rs.at[i], {"row": row_at(i)})

    own_tokens = pltpu.make_async_copy(tok, xg.at[0], own_sem)
    own_tokens.start()
    for role in range(4):
        for g in range(2):
            load(role, g).start()

    barrier = pltpu.get_barrier_semaphore()

    @pl.loop(1, n)
    def _(i):
        pl.semaphore_signal(barrier, inc=1, device_id={"row": row_at(i)}, device_id_type=MESH)

    for peer in shards[:3]:
        pl.semaphore_signal(barrier, inc=1, device_id={"col": peer}, device_id_type=MESH)
    pl.semaphore_wait(barrier, n + 2)

    @pl.loop(1, n)
    def _(i):
        send_tokens(i).start()

    for role in range(4):
        load_down(role).start()

    def project(i, role, store):
        @pl.when(i == 0)
        def _():
            for g in range(2):
                load(role, g).wait()

        x = xg[i]
        for g in range(2):
            @pl.loop(0, F // tile_f)
            def _(t):
                at = pl.ds(pl.multiple_of(t * tile_f, tile_f), tile_f)
                store(g, at, jnp.dot(x, w_v[role, g, :, at], preferred_element_type=f32))

    def partials(i):
        @pl.when(i == 0)
        def _():
            own_tokens.wait()

        @pl.when(i > 0)
        def _():
            send_tokens(i).wait_recv()

        x = xg[i].astype(f32)
        squares = x * x
        lanes = squares[:, :128]
        for c in range(1, width // 128):
            lanes = lanes + squares[:, c * 128:(c + 1) * 128]
        total = jnp.sum(lanes.T, axis=0, keepdims=True)
        q_s[i] = jnp.broadcast_to(total, (8, T))
        xg[i] = (x * gain[...]).astype(bf16)
        for role in range(3):
            send_squares(i, role).start()

        def to_half(which):
            def store(g, at, value):
                a_s[i, which, g, :, at] = value.astype(bf16)
            return store

        def to_chip(g, at, value):
            p_b[g, :, at] = value

        def to_own(g, at, value):
            p_own[lax.rem(i, 2), g, :, at] = value

        project(i, 0, to_half(0))
        send_half(i, 0).start()
        project(i, 1, to_chip)
        send_half(i, 0).wait_recv()
        for g in range(2):
            @pl.loop(0, F // tile_f)
            def _(t):
                at = pl.ds(pl.multiple_of(t * tile_f, tile_f), tile_f)
                b_s[i, g, :, at] = (p_b[g, :, at] + a_r[i, 0, g, :, at].astype(f32)).astype(bf16)
        send_chip(i).start()
        project(i, 2, to_half(1))
        send_half(i, 1).start()
        project(i, 3, to_own)

    def activate(i):
        for role in range(3):
            send_squares(i, role).wait_recv()
        send_half(i, 1).wait_recv()
        send_chip(i).wait_recv()
        total = q_s[i] + q_r[i, 0] + q_r[i, 1] + q_r[i, 2]
        inverse = lax.rsqrt(total / width_total + epsilon)
        inverse = jnp.broadcast_to(inverse[0:1, :], (128, T)).T[:, 0:1]
        slot = lax.rem(i, 2)

        @pl.loop(0, F // tile_f)
        def _(t):
            at = pl.ds(pl.multiple_of(t * tile_f, tile_f), tile_f)
            gate, up = (
                (p_own[slot, g, :, at] + a_r[i, 1, g, :, at].astype(f32) + b_r[i, g, :, at].astype(f32)) * inverse
                for g in range(2)
            )
            hid[i, 3, :, at] = (gate / (1.0 + jnp.exp(-gate)) * up).astype(bf16)

        send_hidden(i, 0).start()
        send_hidden(i, 1).start()

    def lower(i):
        @pl.when(i == 0)
        def _():
            for role in range(4):
                load_down(role).wait()

        send_hidden(i, 0).wait_recv()
        send_hidden(i, 2).start()
        send_hidden(i, 1).wait_recv()
        send_hidden(i, 2).wait_recv()

        @pl.loop(0, width // tile_d)
        def _(t):
            at = pl.ds(pl.multiple_of(t * tile_d, tile_d), tile_d)
            total = jnp.dot(hid[i, 3], wd_v[3, :, at], preferred_element_type=f32)
            for role in range(3):
                total += jnp.dot(hid[i, role], wd_v[role, :, at], preferred_element_type=f32)
            o_s[i, :, at] = total.astype(bf16)

        @pl.when(i > 0)
        def _():
            send_out(i).start()

    @pl.loop(0, n + 2)
    def _(step):
        @pl.when(step < n)
        def _():
            partials(step)

        @pl.when((step >= 1) & (step < n + 1))
        def _():
            activate(step - 1)

        @pl.when(step >= 2)
        def _():
            lower(step - 2)

    @pl.loop(1, n)
    def _(i):
        send_out(i).wait_recv()

    @pl.loop(0, width // tile_d)
    def _(t):
        at = pl.ds(pl.multiple_of(t * tile_d, tile_d), tile_d)
        out[:, at] = lax.fori_loop(
            1, n, lambda i, total: total + o_r[i, :, at].astype(f32), o_s[0, :, at].astype(f32)
        ).astype(bf16)

    @pl.loop(0, n)
    def _(i):
        @pl.when(i > 0)
        def _():
            send_tokens(i).wait_send()
            send_out(i).wait_send()

        send_half(i, 0).wait_send()
        send_half(i, 1).wait_send()
        send_chip(i).wait_send()
        for which in range(3):
            send_hidden(i, which).wait_send()
            send_squares(i, which).wait_send()


def per_device(n, tokens, norm_gain, gate_weight, up_weight, down_weight):
    T, width = tokens.shape
    F = gate_weight.shape[1] // 4
    dma = pltpu.SemaphoreType.DMA
    anywhere = pl.BlockSpec(memory_space=pl.ANY)
    vmem = pl.BlockSpec(memory_space=pltpu.VMEM)
    return pl.pallas_call(
        functools.partial(kernel, n, width * 4),
        out_shape=jax.ShapeDtypeStruct((T, width), bf16),
        in_specs=[anywhere, vmem, anywhere, anywhere, anywhere],
        out_specs=vmem,
        scratch_shapes=[
            pltpu.VMEM((4, 2, width, F), bf16),
            pltpu.VMEM((4, F, width), bf16),
            pltpu.VMEM((n, T, width), bf16),
            pltpu.VMEM((n, 2, 2, T, F), bf16),
            pltpu.VMEM((n, 2, 2, T, F), bf16),
            pltpu.VMEM((n, 2, T, F), bf16),
            pltpu.VMEM((n, 2, T, F), bf16),
            pltpu.VMEM((2, 2, T, F), f32),
            pltpu.VMEM((2, T, F), f32),
            pltpu.VMEM((n, 4, T, F), bf16),
            pltpu.VMEM((n, 8, T), f32),
            pltpu.VMEM((n, 3, 8, T), f32),
            pltpu.VMEM((n, T, width), bf16),
            pltpu.VMEM((n, T, width), bf16),
            dma((3, 4)), dma(()),
            dma((n,)), dma((n,)),
            dma((n, 2)), dma((n, 2)),
            dma((n,)), dma((n,)),
            dma((n, 3)), dma((n, 3)),
            dma((n, 3)), dma((n, 3)),
            dma((n,)), dma((n,)),
        ],
        compiler_params=pltpu.CompilerParams(
            collective_id=0, has_side_effects=True, vmem_limit_bytes=58 * 1024 * 1024
        ),
    )(tokens, norm_gain[None, :], gate_weight, up_weight, down_weight)


def solution(mesh):
    placed = (
        P(("groups", "row"), "col"),
        P("col"),
        P("col", "row"),
        P("col", "row"),
        P("row", "col"),
    )
    return jax.shard_map(
        functools.partial(per_device, mesh.shape["row"]),
        mesh=mesh,
        in_specs=placed,
        out_specs=P(("groups", "row"), "col"),
        check_vma=False,
    )
```

time: 215 us -> 104 us (0.48)
  waiting for transfers between devices: 162 us -> 0 us
  Pallas kernels: 0 us -> 102 us
  matrix products: 24.9 us -> 0 us
  between operations: 13.1 us -> 0.01 us
  blocking collectives: 8.34 us -> 0 us
  other arithmetic: 6.43 us -> 0 us
    pallas_call x0 -> x1, Pallas kernels: none -> 102 us  [per_device(): pl.pallas_call(functools.partial(kernel, n, width * 4), out_shape=jax.Sha...]
    reduce_scatter x2 -> x0, waiting for transfers between devices: 98.6 us -> none  [the longest x1 71.3 us: per_device(): lax.psum_scatter(jnp.dot(block_rows, both_weights, preferred_element_type...]
    all_gather x2 -> x0, waiting for transfers between devices: 63 us -> none  [the longest x1 34.6 us: per_device(): hidden = lax.all_gather(hidden_part, 'col', axis=0, tiled=True)]
    dot_general x2 -> x0, matrix products: 24.9 us -> none  [the longest x1 14.8 us: per_device(): jnp.dot(block_rows, both_weights, preferred_element_type=jnp.float32)]
    psum x1 -> x0, blocking collectives: 8.34 us -> none  [per_device(): total_squares = lax.psum(local_squares, 'col')]
    convert_element_type x3 -> x0, other arithmetic: 5.34 us -> none  [the longest x1 2 us: per_device(): summed = lax.psum_scatter(jnp.dot(block_rows, both_weights, preferred_ele...]
  transfers between devices with their start and end apart: 4 -> 0, of which waited for: 4 -> 0; matrix products, arithmetic and copies ran while one was open for 0% -> 0% of each run, Pallas kernels for 0% -> 0%
where the time goes in v1:
time: 104 us
  Pallas kernels  102 us (98%)
  local copies, waits for them, and re-layouts  1.67 us (2%)
    pallas_call x1, Pallas kernels, per_device(): pl.pallas_call(functools.partial(kernel, n, width * 4), out_shape=jax.Sha...  102 us

profile of v1, /device:TPU:0, one launch (start us, length us, event | category | flops | bytes accessed | tf_op | source)
XLA Modules:
  0.0 103.7 jit_solution(8179836626101004904)
XLA Ops:
  0.0 102.0 %shard_map.55 = bf16[128,1024]{1,0:T(8,128)(2,1)} custom-call(bf16[128,1024]{1,0:T(8,128)(2,1)} %tok.1, f32[1,1024]{1,0:T(1,128)} %bitcast.1, bf16[1024,4096]{1,0:T(8,128)(2,1)} %gate_w.1, bf16[1024,4096]{1,0:T(8,128)(2,1)} %up_w.1, bf16[4096,1024]{1,0:T(8,128)(2,1)} %down_w.1), custom_call_target="tpu_custom_call" | custom-call | tf_op jit(solution)/shard_map/pallas_call | solution.py:242
  102.0 1.7 %copy.7 = bf16[128,1024]{1,0:T(8,128)(2,1)} copy(bf16[128,1024]{1,0:T(8,128)(2,1)} %shard_map.55) | data formatting | bytes 524288

commit v2 on v1

v2 whole, which is shorter than its diff:
```python
import functools
import jax
import jax.numpy as jnp
from jax import lax
from jax.experimental import pallas as pl
from jax.experimental.pallas import tpu as pltpu
from jax.sharding import PartitionSpec as P

epsilon = 1e-05
MESH = pl.DeviceIdType.MESH
f32 = jnp.float32
bf16 = jnp.bfloat16


def remote(src, dst, send, recv, device):
    return pltpu.make_async_remote_copy(
        src_ref=src, dst_ref=dst, send_sem=send, recv_sem=recv, device_id=device, device_id_type=MESH
    )


def kernel(n, width_total, tok, gain, gate_w, up_w, down_w, out,
           w_v, wd_v, xg, a_s, a_r, b_s, b_r, p_own, p_b, hid, q_s, q_r, o_s, o_r, total,
           w_sem, own_sem, t_ss, t_rs, a_ss, a_rs, b_ss, b_rs, h_ss, h_rs, q_ss, q_rs, o_ss, o_rs):
    T, width = tok.shape
    rows = T // 2
    F = gate_w.shape[1] // 4
    tile_f = min(256, F)
    tile_d = min(256, width)
    row = lax.axis_index("row")
    col = lax.axis_index("col")
    hi, lo = col // 2, col % 2
    sibling = hi * 2 + (1 - lo)
    across = (1 - hi) * 2 + lo
    diagonal = (1 - hi) * 2 + (1 - lo)
    shards = (diagonal, across, sibling, col)

    def shift(step):
        late = jnp.where(step == n - 1, n - 1, jnp.where(step == n - 2, 1, step + 1))
        return jnp.where(step == 0, 0, late)

    def row_at(step):
        return lax.rem(row + shift(step), n)

    def row_back(step):
        return lax.rem(row + n - shift(step), n)

    def load(role, g):
        at = pl.ds(pl.multiple_of(shards[role] * F, F), F)
        source = (gate_w, up_w)[g].at[:, at]
        return pltpu.make_async_copy(source, w_v.at[role, g], w_sem.at[g, role])

    def load_down(role):
        at = pl.ds(pl.multiple_of(shards[role] * F, F), F)
        return pltpu.make_async_copy(down_w.at[at, :], wd_v.at[role], w_sem.at[2, role])

    def send_tokens(i):
        return remote(tok, xg.at[i], t_ss.at[i], t_rs.at[i], {"row": row_back(i)})

    def send_half(i, which, g):
        return remote(a_s.at[i, which, g], a_r.at[i, which, g],
                      a_ss.at[i, which, g], a_rs.at[i, which, g], {"col": sibling})

    def send_chip(i, g):
        return remote(b_s.at[i, g], b_r.at[i, g], b_ss.at[i, g], b_rs.at[i, g], {"col": across})

    def send_hidden(i, which, half):
        source, target, device = ((3, 1, across), (3, 2, sibling), (1, 0, sibling))[which]
        at = pl.ds(half * rows, rows)
        return remote(hid.at[i, source, at], hid.at[i, target, at],
                      h_ss.at[i, which, half], h_rs.at[i, which, half], {"col": device})

    def send_squares(i, role):
        return remote(q_s.at[i], q_r.at[i, role], q_ss.at[i, role], q_rs.at[i, role], {"col": shards[role]})

    def send_out(i, half):
        return remote(o_s.at[i, half], o_r.at[i, half], o_ss.at[i, half], o_rs.at[i, half], {"row": row_at(i)})

    own_tokens = pltpu.make_async_copy(tok, xg.at[0], own_sem)
    own_tokens.start()
    for g in range(2):
        for role in range(2):
            load(role, g).start()

    barrier = pltpu.get_barrier_semaphore()

    @pl.loop(1, n)
    def _(i):
        pl.semaphore_signal(barrier, inc=1, device_id={"row": row_at(i)}, device_id_type=MESH)

    for peer in shards[:3]:
        pl.semaphore_signal(barrier, inc=1, device_id={"col": peer}, device_id_type=MESH)
    pl.semaphore_wait(barrier, n + 2)

    if n > 1:
        send_tokens(1).start()

    for role in range(2, 4):
        for g in range(2):
            load(role, g).start()
    for role in range(4):
        load_down(role).start()

    def project(i, role, g, store):
        @pl.when(i == 0)
        def _():
            load(role, g).wait()

        x = xg[i]

        @pl.loop(0, F // tile_f)
        def _(t):
            at = pl.ds(pl.multiple_of(t * tile_f, tile_f), tile_f)
            store(g, at, jnp.dot(x, w_v[role, g, :, at], preferred_element_type=f32))

    def partials(i):
        @pl.when(i == 0)
        def _():
            own_tokens.wait()

        @pl.when(i > 0)
        def _():
            send_tokens(i).wait_recv()

        @pl.when((i > 0) & (i + 1 < n))
        def _():
            send_tokens(i + 1).start()

        x = xg[i].astype(f32)
        squares = x * x
        lanes = squares[:, :128]
        for c in range(1, width // 128):
            lanes = lanes + squares[:, c * 128:(c + 1) * 128]
        q_s[i] = jnp.broadcast_to(jnp.sum(lanes.T, axis=0, keepdims=True), (8, T))
        xg[i] = (x * gain[...]).astype(bf16)
        for role in range(3):
            send_squares(i, role).start()

        def to_half(which):
            def store(g, at, value):
                a_s[i, which, g, :, at] = value.astype(bf16)
            return store

        def to_chip(g, at, value):
            p_b[g, :, at] = value

        def to_own(g, at, value):
            p_own[lax.rem(i, 2), g, :, at] = value

        for g in range(2):
            project(i, 0, g, to_half(0))
            send_half(i, 0, g).start()
            project(i, 1, g, to_chip)
            send_half(i, 0, g).wait_recv()

            @pl.loop(0, F // tile_f)
            def _(t):
                at = pl.ds(pl.multiple_of(t * tile_f, tile_f), tile_f)
                b_s[i, g, :, at] = (p_b[g, :, at] + a_r[i, 0, g, :, at].astype(f32)).astype(bf16)

            send_chip(i, g).start()

        for g in range(2):
            project(i, 2, g, to_half(1))
            send_half(i, 1, g).start()
        for g in range(2):
            project(i, 3, g, to_own)

    def activate(i):
        for role in range(3):
            send_squares(i, role).wait_recv()
        for g in range(2):
            send_half(i, 1, g).wait_recv()
            send_chip(i, g).wait_recv()
        all_squares = q_s[i] + q_r[i, 0] + q_r[i, 1] + q_r[i, 2]
        inverse = lax.rsqrt(all_squares / width_total + epsilon)
        inverse = jnp.broadcast_to(inverse[0:1, :], (128, T)).T[:, 0:1]
        slot = lax.rem(i, 2)

        for half in range(2):
            part = pl.ds(half * rows, rows)
            factor = inverse[half * rows:(half + 1) * rows]

            @pl.loop(0, F // tile_f)
            def _(t):
                at = pl.ds(pl.multiple_of(t * tile_f, tile_f), tile_f)
                gate, up = (
                    (p_own[slot, g, part, at] + a_r[i, 1, g, part, at].astype(f32)
                     + b_r[i, g, part, at].astype(f32)) * factor
                    for g in range(2)
                )
                hid[i, 3, part, at] = (gate / (1.0 + jnp.exp(-gate)) * up).astype(bf16)

            send_hidden(i, 0, half).start()
            send_hidden(i, 1, half).start()

    def lower(i):
        @pl.when(i == 0)
        def _():
            for role in range(4):
                load_down(role).wait()

        for half in range(2):
            send_hidden(i, 1, half).wait_recv()

        def product(role, part, at):
            return jnp.dot(hid[i, role, part], wd_v[role, :, at], preferred_element_type=f32)

        @pl.loop(0, width // tile_d)
        def _(t):
            at = pl.ds(pl.multiple_of(t * tile_d, tile_d), tile_d)
            every = pl.ds(0, T)
            total[:, at] = product(3, every, at) + product(2, every, at)

        for half in range(2):
            part = pl.ds(half * rows, rows)
            send_hidden(i, 0, half).wait_recv()
            send_hidden(i, 2, half).start()

            @pl.loop(0, width // tile_d)
            def _(t):
                at = pl.ds(pl.multiple_of(t * tile_d, tile_d), tile_d)
                total[part, at] += product(1, part, at)

            send_hidden(i, 2, half).wait_recv()

            @pl.loop(0, width // tile_d)
            def _(t):
                at = pl.ds(pl.multiple_of(t * tile_d, tile_d), tile_d)
                o_s[i, half, :, at] = (total[part, at] + product(0, part, at)).astype(bf16)

            @pl.when(i > 0)
            def _():
                send_out(i, half).start()

    @pl.loop(0, n + 2)
    def _(step):
        @pl.when(step < n)
        def _():
            partials(step)

        @pl.when((step >= 1) & (step < n + 1))
        def _():
            activate(step - 1)

        @pl.when(step >= 2)
        def _():
            lower(step - 2)

    for half in range(2):
        @pl.loop(1, n)
        def _(i):
            send_out(i, half).wait_recv()

        @pl.loop(0, width // tile_d)
        def _(t):
            at = pl.ds(pl.multiple_of(t * tile_d, tile_d), tile_d)
            out[pl.ds(half * rows, rows), at] = lax.fori_loop(
                1, n, lambda i, so_far: so_far + o_r[i, half, :, at].astype(f32), o_s[0, half, :, at].astype(f32)
            ).astype(bf16)

    @pl.loop(0, n)
    def _(i):
        @pl.when(i > 0)
        def _():
            send_tokens(i).wait_send()
            send_out(i, 0).wait_send()
            send_out(i, 1).wait_send()

        for piece in range(2):
            send_half(i, 0, piece).wait_send()
            send_half(i, 1, piece).wait_send()
            send_chip(i, piece).wait_send()
        for which in range(3):
            for half in range(2):
                send_hidden(i, which, half).wait_send()
            send_squares(i, which).wait_send()


def per_device(n, tokens, norm_gain, gate_weight, up_weight, down_weight):
    T, width = tokens.shape
    F = gate_weight.shape[1] // 4
    dma = pltpu.SemaphoreType.DMA
    anywhere = pl.BlockSpec(memory_space=pl.ANY)
    vmem = pl.BlockSpec(memory_space=pltpu.VMEM)
    return pl.pallas_call(
        functools.partial(kernel, n, width * 4),
        out_shape=jax.ShapeDtypeStruct((T, width), bf16),
        in_specs=[anywhere, vmem, anywhere, anywhere, anywhere],
        out_specs=vmem,
        scratch_shapes=[
            pltpu.VMEM((4, 2, width, F), bf16),
            pltpu.VMEM((4, F, width), bf16),
            pltpu.VMEM((n, T, width), bf16),
            pltpu.VMEM((n, 2, 2, T, F), bf16),
            pltpu.VMEM((n, 2, 2, T, F), bf16),
            pltpu.VMEM((n, 2, T, F), bf16),
            pltpu.VMEM((n, 2, T, F), bf16),
            pltpu.VMEM((2, 2, T, F), f32),
            pltpu.VMEM((2, T, F), f32),
            pltpu.VMEM((n, 4, T, F), bf16),
            pltpu.VMEM((n, 8, T), f32),
            pltpu.VMEM((n, 3, 8, T), f32),
            pltpu.VMEM((n, 2, T // 2, width), bf16),
            pltpu.VMEM((n, 2, T // 2, width), bf16),
            pltpu.VMEM((T, width), f32),
            dma((3, 4)), dma(()),
            dma((n,)), dma((n,)),
            dma((n, 2, 2)), dma((n, 2, 2)),
            dma((n, 2)), dma((n, 2)),
            dma((n, 3, 2)), dma((n, 3, 2)),
            dma((n, 3)), dma((n, 3)),
            dma((n, 2)), dma((n, 2)),
        ],
        compiler_params=pltpu.CompilerParams(
            collective_id=0, has_side_effects=True, vmem_limit_bytes=58 * 1024 * 1024
        ),
    )(tokens, norm_gain[None, :], gate_weight, up_weight, down_weight)


def solution(mesh):
    placed = (
        P(("groups", "row"), "col"),
        P("col"),
        P("col", "row"),
        P("col", "row"),
        P("row", "col"),
    )
    return jax.shard_map(
        functools.partial(per_device, mesh.shape["row"]),
        mesh=mesh,
        in_specs=placed,
        out_specs=P(("groups", "row"), "col"),
        check_vma=False,
    )
```

time: 104 us -> 92.4 us (0.89)
  Pallas kernels: 102 us -> 90.6 us
    pallas_call x1, Pallas kernels: 102 us -> 90.6 us  [per_device(): pl.pallas_call(functools.partial(kernel, n, width * 4), out_shape=jax.Sha...]
where the time goes in v2:
time: 92.4 us; the launch traced here: 92.2 us
  Pallas kernels  90.6 us (98%)
  local copies, waits for them, and re-layouts  1.67 us (2%)
    pallas_call x1, Pallas kernels, per_device(): pl.pallas_call(functools.partial(kernel, n, width * 4), out_shape=jax.Sha...  90.6 us

profile of v2, /device:TPU:0, one launch (start us, length us, event | category | flops | bytes accessed | tf_op | source)
XLA Modules:
  0.0 92.2 jit_solution(4117462405358578584)
XLA Ops:
  0.0 90.6 %shard_map.55 = bf16[128,1024]{1,0:T(8,128)(2,1)} custom-call(bf16[128,1024]{1,0:T(8,128)(2,1)} %tok.1, f32[1,1024]{1,0:T(1,128)} %bitcast.1, bf16[1024,4096]{1,0:T(8,128)(2,1)} %gate_w.1, bf16[1024,4096]{1,0:T(8,128)(2,1)} %up_w.1, bf16[4096,1024]{1,0:T(8,128)(2,1)} %down_w.1), custom_call_target="tpu_custom_call" | custom-call | tf_op jit(solution)/shard_map/pallas_call | solution.py:285
  90.6 1.7 %copy.7 = bf16[128,1024]{1,0:T(8,128)(2,1)} copy(bf16[128,1024]{1,0:T(8,128)(2,1)} %shard_map.55) | data formatting | bytes 524288

commit v3 on v2

--- a/solution.py
+++ b/solution.py
@@ -19,13 +19,13 @@
 
 
 def kernel(n, width_total, tok, gain, gate_w, up_w, down_w, out,
-           w_v, wd_v, xg, a_s, a_r, b_s, b_r, p_own, p_b, hid, q_s, q_r, o_s, o_r, total,
+           w_v, wd_v, xg, a_s, a_r, b_s, b_r, p_own, p_b, hid, q_s, q_r, o_s, o_r, total, xs,
            w_sem, own_sem, t_ss, t_rs, a_ss, a_rs, b_ss, b_rs, h_ss, h_rs, q_ss, q_rs, o_ss, o_rs):
     T, width = tok.shape
     rows = T // 2
     F = gate_w.shape[1] // 4
-    tile_f = min(256, F)
-    tile_d = min(256, width)
+    tile_f = min(512, F)
+    tile_d = min(512, width)
     row = lax.axis_index("row")
     col = lax.axis_index("col")
     hi, lo = col // 2, col % 2
@@ -105,35 +105,37 @@
         def _():
             load(role, g).wait()
 
-        x = xg[i]
+        x = xs[...]
 
         @pl.loop(0, F // tile_f)
         def _(t):
             at = pl.ds(pl.multiple_of(t * tile_f, tile_f), tile_f)
             store(g, at, jnp.dot(x, w_v[role, g, :, at], preferred_element_type=f32))
 
-    def partials(i):
-        @pl.when(i == 0)
-        def _():
-            own_tokens.wait()
-
-        @pl.when(i > 0)
-        def _():
-            send_tokens(i).wait_recv()
-
-        @pl.when((i > 0) & (i + 1 < n))
-        def _():
-            send_tokens(i + 1).start()
-
+    def squares_of(i):
         x = xg[i].astype(f32)
         squares = x * x
         lanes = squares[:, :128]
         for c in range(1, width // 128):
             lanes = lanes + squares[:, c * 128:(c + 1) * 128]
         q_s[i] = jnp.broadcast_to(jnp.sum(lanes.T, axis=0, keepdims=True), (8, T))
-        xg[i] = (x * gain[...]).astype(bf16)
         for role in range(3):
             send_squares(i, role).start()
+
+    def partials(i):
+        @pl.when(i == 0)
+        def _():
+            own_tokens.wait()
+
+        @pl.when(i > 0)
+        def _():
+            send_tokens(i).wait_recv()
+
+        @pl.when((i > 0) & (i + 1 < n))
+        def _():
+            send_tokens(i + 1).start()
+
+        xs[...] = (xg[i].astype(f32) * gain[...]).astype(bf16)
 
         def to_half(which):
             def store(g, at, value):
@@ -159,6 +161,7 @@
 
             send_chip(i, g).start()
 
+        squares_of(i)
         for g in range(2):
             project(i, 2, g, to_half(1))
             send_half(i, 1, g).start()
@@ -303,6 +306,7 @@
             pltpu.VMEM((n, 2, T // 2, width), bf16),
             pltpu.VMEM((n, 2, T // 2, width), bf16),
             pltpu.VMEM((T, width), f32),
+            pltpu.VMEM((T, width), bf16),
             dma((3, 4)), dma(()),
             dma((n,)), dma((n,)),
             dma((n, 2, 2)), dma((n, 2, 2)),

time: 92.4 us -> 91.3 us (0.988)
  Pallas kernels: 90.6 us -> 89.4 us
    pallas_call x1, Pallas kernels: 90.6 us -> 89.4 us  [per_device(): pl.pallas_call(functools.partial(kernel, n, width * 4), out_shape=jax.Sha...]
where the time goes in v3:
time: 91.3 us; the launch traced here: 91.1 us
  Pallas kernels  89.4 us (98%)
  local copies, waits for them, and re-layouts  1.67 us (2%)
    pallas_call x1, Pallas kernels, per_device(): pl.pallas_call(functools.partial(kernel, n, width * 4), out_shape=jax.Sha...  89.4 us

profile of v3, /device:TPU:0, one launch (start us, length us, event | category | flops | bytes accessed | tf_op | source)
XLA Modules:
  0.0 91.1 jit_solution(14296205791291318247)
XLA Ops:
  0.0 89.4 %shard_map.55 = bf16[128,1024]{1,0:T(8,128)(2,1)} custom-call(bf16[128,1024]{1,0:T(8,128)(2,1)} %tok.1, f32[1,1024]{1,0:T(1,128)} %bitcast.1, bf16[1024,4096]{1,0:T(8,128)(2,1)} %gate_w.1, bf16[1024,4096]{1,0:T(8,128)(2,1)} %up_w.1, bf16[4096,1024]{1,0:T(8,128)(2,1)} %down_w.1), custom_call_target="tpu_custom_call" | custom-call | tf_op jit(solution)/shard_map/pallas_call | solution.py:288
  89.4 1.7 %copy.7 = bf16[128,1024]{1,0:T(8,128)(2,1)} copy(bf16[128,1024]{1,0:T(8,128)(2,1)} %shard_map.55) | data formatting | bytes 524288
